TPU v7x, 512 devices: a whole 4x4x16 slice. The times are simulated.
512 devices in a mesh: section: 32 (over x, z_lo, core), tp: 16 (over y, z_hi).
Axes of the slice: x: 4, y: 4, z: 16 (z_hi: 4, z_lo: 4; z = z_hi * 4 + z_lo), core: 2. Of those that a mesh axis runs over, the one named last changes fastest.
Arguments:
- held_query: bfloat16 [32, 1024, 64, 128], P('section', 'tp'), may hold values from -6 to 6
- held_key: bfloat16 [32, 1024, 16, 128], P('section', None, 'tp'), may hold values from -6 to 6
- held_value: bfloat16 [32, 1024, 16, 128], P('section', None, 'tp'), may hold values from -6 to 6
- grad_out: bfloat16 [32, 1024, 64, 128], P('section', None, 'tp'), may hold values from -6 to 6
Outputs:
- grad_query: bfloat16 [32, 1024, 64, 128], P('section', None, 'tp')
- grad_key: bfloat16 [32, 1024, 16, 128], P('section', None, 'tp')
- grad_value: bfloat16 [32, 1024, 16, 128], P('section', None, 'tp')
All inputs are finite; a program needn't handle non-finite values.
Results may differ from a plain program's by a relative error of at most 0.0064.
Values may be sent and summed in bfloat16 or wider, within the bound.
A program may use at most 64 MiB of HBM per device.

v0:
```python
import functools

import jax
import jax.numpy as jnp
from jax import lax
from jax.experimental import pallas as pl
from jax.experimental.pallas import tpu as pltpu
from jax.sharding import PartitionSpec as P

MESH = pl.DeviceIdType.MESH
LOG2E = 1.4426950408889634
CONTRACT_LAST = (((1,), (1,)), ((), ()))


def local_wait(ref, sem):
    pltpu.make_async_copy(ref, ref, sem).wait()


def kernel(
    sections, parts, tokens, group,
    q_ref, k_ref, v_ref, g_ref,
    dq_ref, dk_ref, dv_ref,
    q_in, k_in, v_in, g_in, k_turned, dk_sum, dv_sum,
    q_sem, g_sem, k_sem, v_sem, q_out_sem, g_out_sem, k_out_sem, v_out_sem,
):
    s = lax.axis_index("section")
    t = lax.axis_index("tp")
    rows = tokens * group
    length = parts * tokens
    width = q_ref.shape[-1]
    scale = width ** (-0.5)
    works = s < sections - 1
    partner = sections - 2 - s
    alone = partner == s
    gives = s > 0

    def at_step(step):
        return lax.rem(5 * step + s, parts)

    def block(index):
        return pl.ds(pl.multiple_of(index * rows, rows), rows)

    barrier = pltpu.get_barrier_semaphore()

    def greet(index, carry):
        @pl.when(jnp.logical_and(works, jnp.logical_not(jnp.logical_and(alone, index == t))))
        def _():
            pl.semaphore_signal(barrier, inc=1, device_id=(partner, index), device_id_type=MESH)
        return carry

    lax.fori_loop(0, parts, greet, 0)

    @pl.when(works)
    def _():
        pl.semaphore_signal(barrier, inc=1, device_id=(s + 1, t), device_id_type=MESH)

    pl.semaphore_wait(
        barrier,
        jnp.where(works, parts, 0) - jnp.where(alone, 1, 0) + jnp.where(gives, 1, 0),
    )

    def hand_over(source, target, out_sem, in_sem):
        @pl.when(jnp.logical_and(works, jnp.logical_not(alone)))
        def _():
            pltpu.make_async_remote_copy(
                src_ref=source, dst_ref=target, send_sem=out_sem, recv_sem=in_sem,
                device_id=(partner, t), device_id_type=MESH,
            ).start()

        @pl.when(alone)
        def _():
            pltpu.make_async_copy(source, target, in_sem).start()

    hand_over(k_ref, k_in, k_out_sem, k_sem)
    hand_over(v_ref, v_in, v_out_sem, v_sem)

    def send(step, carry):
        @pl.when(gives)
        def _():
            theirs = lax.rem(lax.rem(5 * step + s - 1, parts) + t, parts)
            pltpu.make_async_remote_copy(
                src_ref=g_ref.at[block(theirs)],
                dst_ref=g_in.at[block(theirs)],
                send_sem=g_out_sem,
                recv_sem=g_sem.at[theirs],
                device_id=(s - 1, t),
                device_id_type=MESH,
            ).start()

        @pl.when(works)
        def _():
            shift = lax.rem(5 * step + partner, parts)
            to = lax.rem(t + parts - shift, parts)
            itself = jnp.logical_and(alone, to == t)

            @pl.when(jnp.logical_not(itself))
            def _():
                pltpu.make_async_remote_copy(
                    src_ref=q_ref.at[block(to)],
                    dst_ref=q_in.at[block(t)],
                    send_sem=q_out_sem,
                    recv_sem=q_sem.at[t],
                    device_id=(partner, to),
                    device_id_type=MESH,
                ).start()

            @pl.when(itself)
            def _():
                pltpu.make_async_copy(q_ref.at[block(to)], q_in.at[block(t)], q_sem.at[t]).start()

        return carry

    lax.fori_loop(0, parts, send, 0)

    dk_sum[...] = jnp.zeros_like(dk_sum)
    dv_sum[...] = jnp.zeros_like(dv_sum)

    def backward(index, keys):
        here = block(index)
        query, upstream = q_in[here, :], g_in[here, :]
        key, value = k_in[:keys, :], v_in[:keys, :]
        scores = lax.dot_general(key, query, CONTRACT_LAST, preferred_element_type=jnp.float32)
        token = index * tokens + lax.broadcasted_iota(jnp.int32, (keys, rows), 1) // group
        seen = lax.broadcasted_iota(jnp.int32, (keys, rows), 0) <= token
        scores = jnp.where(seen, scores, -1e30)
        top = jnp.max(scores, axis=0, keepdims=True)
        weights = jnp.exp2((scores - top) * (scale * LOG2E))
        share = 1.0 / jnp.sum(weights, axis=0, keepdims=True)
        probs = weights * share
        dv_sum[:keys, :] += jnp.dot(
            probs.astype(jnp.bfloat16), upstream, preferred_element_type=jnp.float32
        )
        grad_probs = lax.dot_general(
            value, upstream, CONTRACT_LAST, preferred_element_type=jnp.float32
        )
        delta = jnp.sum(probs * grad_probs, axis=0, keepdims=True)
        grad_scores = (probs * (grad_probs - delta) * scale).astype(jnp.bfloat16)
        dk_sum[:keys, :] += jnp.dot(grad_scores, query, preferred_element_type=jnp.float32)
        turned = jnp.dot(k_turned[:, :keys], grad_scores, preferred_element_type=jnp.float32)
        dq_ref[here, :] = turned.T.astype(dq_ref.dtype)

    @pl.when(works)
    def _():
        local_wait(k_in, k_sem)
        local_wait(v_in, v_sem)
        k_turned[...] = k_in[...].T

        def take(step, carry):
            index = lax.rem(at_step(step) + t, parts)
            local_wait(q_in.at[block(index)], q_sem.at[index])
            local_wait(g_in.at[block(index)], g_sem.at[index])
            spans = 4
            for span in range(spans):
                @pl.when(index // (parts // spans) == span)
                def _():
                    backward(index, (span + 1) * length // spans)
            return carry

        lax.fori_loop(0, parts, take, 0)

    @pl.when(jnp.logical_not(works))
    def _():
        dq_ref[...] = jnp.zeros_like(dq_ref)

    dk_ref[...] = dk_sum[...].astype(dk_ref.dtype)
    dv_ref[...] = dv_sum[...].astype(dv_ref.dtype)

    @pl.when(jnp.logical_and(works, jnp.logical_not(alone)))
    def _():
        local_wait(k_ref, k_out_sem)
        local_wait(v_ref, v_out_sem)
        local_wait(q_ref, q_out_sem)

    @pl.when(alone)
    def _():
        local_wait(q_ref.at[pl.ds(0, (parts - 1) * rows)], q_out_sem)

    @pl.when(gives)
    def _():
        local_wait(g_ref, g_out_sem)


def local(held_query, held_key, held_value, grad_out):
    sections, parts = lax.axis_size("section"), lax.axis_size("tp")
    _, tokens, heads, width = held_query.shape
    length = held_key.shape[1]
    group = heads // parts
    query = held_query.reshape(tokens, parts, group, width)
    query = jnp.swapaxes(query, 0, 1).reshape(parts * tokens * group, width)
    key = held_key.reshape(length, width)
    value = held_value.reshape(length, width)
    upstream = grad_out.reshape(length * group, width)
    tall, short = upstream.shape, key.shape
    grad_q, grad_k, grad_v = pl.pallas_call(
        functools.partial(kernel, sections, parts, tokens, group),
        out_shape=(
            jax.ShapeDtypeStruct(tall, jnp.bfloat16),
            jax.ShapeDtypeStruct(short, jnp.bfloat16),
            jax.ShapeDtypeStruct(short, jnp.bfloat16),
        ),
        in_specs=[pl.BlockSpec(memory_space=pl.ANY)] * 4,
        out_specs=[pl.BlockSpec(memory_space=pltpu.VMEM)] * 3,
        scratch_shapes=[
            pltpu.VMEM(tall, jnp.bfloat16),
            pltpu.VMEM(short, jnp.bfloat16),
            pltpu.VMEM(short, jnp.bfloat16),
            pltpu.VMEM(tall, jnp.bfloat16),
            pltpu.VMEM((width, length), jnp.bfloat16),
            pltpu.VMEM(short, jnp.float32),
            pltpu.VMEM(short, jnp.float32),
            pltpu.SemaphoreType.DMA((parts,)),
            pltpu.SemaphoreType.DMA((parts,)),
        ]
        + [pltpu.SemaphoreType.DMA] * 6,
        compiler_params=pltpu.CompilerParams(
            collective_id=0, has_side_effects=True, vmem_limit_bytes=48 * 1024 * 1024
        ),
    )(query, key, value, upstream)
    return (
        grad_q.reshape(grad_out.shape),
        grad_k.reshape(held_key.shape),
        grad_v.reshape(held_value.shape),
    )


def solution(mesh):
    placed = (
        P("section", "tp", None, None),
        P("section", None, "tp", None),
        P("section", None, "tp", None),
        P("section", None, "tp", None),
    )
    return jax.shard_map(
        local,
        mesh=mesh,
        in_specs=placed,
        out_specs=(
            P("section", None, "tp", None),
            P("section", None, "tp", None),
            P("section", None, "tp", None),
        ),
        check_vma=False,
    )
```

profile of v0, /device:TPU:38, one launch (start us, length us, event | category | flops | bytes accessed | tf_op | source)
XLA Modules:
  0.0 105.7 jit_solution(1147342570768941048)
XLA Ops:
  0.6 0.0 copy-start
  0.6 0.0 copy-start.1
  0.7 0.0 copy-start.2
  0.7 1.8 %copy.7 = bf16[64,16,4,128]{3,2,0,1:T(4,128)(2,1)S(1)} copy(bf16[64,16,4,128]{3,2,1,0:T(4,128)(2,1)} %bitcast.17) | data formatting | bytes 2097152 | tf_op jit(solution)/shard_map/reshape | solution.py:188
  2.5 0.0 copy-done
  2.5 0.0 copy-done.1
  2.5 0.0 copy-done.2
  2.5 100.8 %shard_map.67 = (bf16[4096,128]{1,0:T(8,128)(2,1)S(1)}, bf16[1024,128]{1,0:T(8,128)(2,1)S(1)}, bf16[1024,128]{1,0:T(8,128)(2,1)S(1)}) custom-call(bf16[4096,128]{1,0:T(8,128)(2,1)S(1)} %bitcast.10, bf16[1024,128]{1,0:T(8,128)(2,1)S(1)} %bitcast.13, bf16[1024,128]{1,0:T(8,128)(2,1)S(1)} %bitcast.14, bf16[4096,128]{1,0:T(8,128)(2,1)S(1)} %bitcast.11), custom_call_target="tpu_custom_call" | custom-call | tf_op jit(solution)/shard_map/pallas_call | solution.py:194
  103.3 1.0 copy.11
  104.3 0.7 copy.12
  105.0 0.7 copy.13
Async XLA Ops:
  0.6 1.9 %copy-start = (bf16[1,1024,4,128]{3,2,1,0:T(4,128)(2,1)S(1)}, bf16[1,1024,4,128]{3,2,1,0:T(4,128)(2,1)}, u32[]{:S(2)}) copy-start(bf16[1,1024,4,128]{3,2,1,0:T(4,128)(2,1)} %param.7) | copy-start | bytes 3145732
  0.6 1.9 %copy-start.1 = (bf16[1,1024,1,128]{3,1,2,0:T(8,128)(2,1)S(1)}, bf16[1,1024,1,128]{3,1,2,0:T(8,128)(2,1)}, u32[]{:S(2)}) copy-start(bf16[1,1024,1,128]{3,1,2,0:T(8,128)(2,1)} %param.5) | copy-start | bytes 786436
  0.7 1.9 %copy-start.2 = (bf16[1,1024,1,128]{3,1,2,0:T(8,128)(2,1)S(1)}, bf16[1,1024,1,128]{3,1,2,0:T(8,128)(2,1)}, u32[]{:S(2)}) copy-start(bf16[1,1024,1,128]{3,1,2,0:T(8,128)(2,1)} %param.6) | copy-start | bytes 786436
where the time goes:
time: 106 us
  Pallas kernels  101 us (95%)
  local copies, waits for them, and re-layouts  4.2 us (4%)
    pallas_call x1, Pallas kernels, local(): pl.pallas_call(functools.partial(kernel, sections, parts, tokens, group),...  101 us
    unnamed x9, local copies, waits for them, and re-layouts  2.39 us

commit v1 on v0

v1 whole, which is shorter than its diff:
```python
import functools

import jax
import jax.numpy as jnp
from jax import lax
from jax.experimental import pallas as pl
from jax.experimental.pallas import tpu as pltpu
from jax.sharding import PartitionSpec as P

MESH = pl.DeviceIdType.MESH
LOG2E = 1.4426950408889634
SIZE_Z = 4
LATEST = 2
ORDER = (0, 1, 3, 2)
FIRST = (16, 8, 0, 4)
CONTRACT_LAST = (((1,), (1,)), ((), ()))


def local_wait(ref, sem):
    pltpu.make_async_copy(ref, ref, sem).wait()


def kernel(
    sections, parts, tokens, group,
    q_ref, k_ref, v_ref, g_ref,
    dq_ref, dk_ref, dv_ref,
    q_in, k_in, v_in, g_in, q_mid, k_turned, dk_sum, dv_sum,
    q_sem, g_sem, k_sem, v_sem, q_mid_sem, q_out_sem, g_out_sem, k_out_sem, v_out_sem, q_on_sem, all_in,
):
    s = lax.axis_index("section")
    t = lax.axis_index("tp")
    rows = tokens * group
    length = parts * tokens
    width = q_ref.shape[-1]
    scale = width ** (-0.5)
    size_y = parts // SIZE_Z
    y, z = t // SIZE_Z, lax.rem(t, SIZE_Z)
    works = s < sections - 1
    gives = s > 0
    partner = sections - 2 - s
    alone = partner == s
    level = jnp.logical_and(works, lax.rem(s, 4) == 3)
    leads = z == LATEST

    def at(z, y):
        return y * SIZE_Z + z

    def block(index):
        return pl.ds(pl.multiple_of(index * rows, rows), rows)

    def no(condition):
        return jnp.logical_not(condition)

    def both(one, other):
        return jnp.logical_and(one, other)

    barrier = pltpu.get_barrier_semaphore()

    def greet(condition, section, part):
        @pl.when(condition)
        def _():
            pl.semaphore_signal(barrier, inc=1, device_id=(section, part), device_id_type=MESH)

    for other in range(size_y):
        greet(both(works, no(both(alone, y == other))), partner, at(z, other))
        greet(both(works, no(leads)), partner, at(LATEST, other))
    greet(no(leads), s, at(LATEST, y))
    greet(works, s + 1, t)
    own = jnp.where(works, size_y, 0) - jnp.where(alone, 1, 0) + jnp.where(gives, 1, 0)
    others = jnp.where(works, parts - size_y, 0) + SIZE_Z - 1
    pl.semaphore_wait(barrier, own + jnp.where(leads, others, 0))

    @pl.when(leads)
    def _():
        for other in range(SIZE_Z):
            if other != LATEST:
                pl.semaphore_signal(all_in, inc=1, device_id=(s, at(other, y)), device_id_type=MESH)

    def push(condition, origin, target, out_sem, in_sem, section, part):
        @pl.when(condition)
        def _():
            pltpu.make_async_remote_copy(
                src_ref=origin, dst_ref=target, send_sem=out_sem, recv_sem=in_sem,
                device_id=(section, part), device_id_type=MESH,
            ).start()

    def hand_over(origin, target, out_sem, in_sem):
        push(both(works, no(alone)), origin, target, out_sem, in_sem, partner, t)

        @pl.when(alone)
        def _():
            pltpu.make_async_copy(origin, target, in_sem).start()

    def taken(step, section):
        upper = lax.rem(section, 2 * SIZE_Z) >= SIZE_Z
        same = lax.rem(section, 4) == 3
        turned = step // size_y
        apart = jnp.where(
            turned == 0,
            jnp.where(same, 0, jnp.where(upper, 1, 3)),
            jnp.where(
                turned == 1,
                jnp.where(same, 1, 2),
                jnp.where(
                    turned == 2,
                    jnp.where(same, 3, 0),
                    jnp.where(same, 2, jnp.where(upper, 3, 1)),
                ),
            ),
        )
        return at(lax.rem(z + apart, SIZE_Z), lax.rem(y + size_y - lax.rem(step, size_y), size_y))

    def send_upstream(step, carry):
        index = taken(step, s - 1)
        push(gives, g_ref.at[block(index)], g_in.at[block(index)], g_out_sem, g_sem.at[index], s - 1, t)
        return carry

    def send_query(to):
        itself = both(alone, to == t)
        push(
            both(works, no(itself)),
            q_ref.at[block(to)], q_in.at[block(t)], q_out_sem, q_sem.at[t], partner, to,
        )

        @pl.when(both(works, itself))
        def _():
            pltpu.make_async_copy(q_ref.at[block(to)], q_in.at[block(t)], q_sem.at[t]).start()

    def detour(to_z, to_y):
        return both(level, both(lax.rem(to_z + SIZE_Z - z, SIZE_Z) == 2, lax.rem(y + to_y, 2) == 0))

    def send_beside(step, carry):
        send_query(at(z, lax.rem(y + step, size_y)))
        return carry

    def send_round(step, carry):
        to_y = lax.rem(y + 2 * step, size_y)
        to_z = lax.rem(z + 2, SIZE_Z)
        slot = y // 2
        push(
            level, q_ref.at[block(at(to_z, to_y))], q_mid.at[block(slot)], q_out_sem, q_mid_sem.at[slot],
            partner, at(lax.rem(z + 1, SIZE_Z), to_y),
        )
        return carry

    def send_across(step, carry):
        turn = step // size_y
        to_z = jnp.where(turn == 0, ORDER[0], jnp.where(turn == 1, ORDER[1], jnp.where(turn == 2, ORDER[2], ORDER[3])))
        to_y = lax.rem(y + step, size_y)

        @pl.when(both(to_z != z, no(detour(to_z, to_y))))
        def _():
            send_query(at(to_z, to_y))

        return carry

    def send_pair():
        hand_over(k_ref, k_in, k_out_sem, k_sem)
        hand_over(v_ref, v_in, v_out_sem, v_sem)

    first = jnp.where(z == 0, FIRST[0], jnp.where(z == 1, FIRST[1], jnp.where(z == 2, FIRST[2], FIRST[3])))

    @pl.when(no(leads))
    def _():
        send_pair()
        lax.fori_loop(0, first, send_upstream, 0)
        lax.fori_loop(0, size_y, send_beside, 0)
        pl.semaphore_wait(all_in, 1)

    lax.fori_loop(0, 2, send_round, 0)
    lax.fori_loop(0, size_y, send_across, 0)

    @pl.when(leads)
    def _():
        send_pair()

    lax.fori_loop(size_y, 2 * size_y, send_across, 0)

    @pl.when(leads)
    def _():
        lax.fori_loop(0, size_y, send_beside, 0)

    lax.fori_loop(2 * size_y, parts, send_across, 0)

    lax.fori_loop(jnp.where(leads, 0, first), parts, send_upstream, 0)

    @pl.when(level)
    def _():
        def on(slot, carry):
            from_y = 2 * slot + lax.rem(y, 2)
            sender = at(lax.rem(z + SIZE_Z - 1, SIZE_Z), from_y)
            local_wait(q_mid.at[block(slot)], q_mid_sem.at[slot])
            push(
                level, q_mid.at[block(slot)], q_in.at[block(sender)], q_on_sem, q_sem.at[sender],
                s, at(lax.rem(z + 1, SIZE_Z), y),
            )
            return carry

        lax.fori_loop(0, 2, on, 0)

    dk_sum[...] = jnp.zeros_like(dk_sum)
    dv_sum[...] = jnp.zeros_like(dv_sum)

    def backward(index, keys):
        here = block(index)
        query, upstream = q_in[here, :], g_in[here, :]
        span = length // 4
        pieces = keys // span
        token = index * tokens - (keys - span) + lax.broadcasted_iota(jnp.int32, (span, rows), 1) // group
        seen = lax.broadcasted_iota(jnp.int32, (span, rows), 0) <= token
        scores = []
        for piece in range(pieces):
            part = lax.dot_general(
                k_in[piece * span : (piece + 1) * span, :], query, CONTRACT_LAST, preferred_element_type=jnp.float32
            )
            scores.append(jnp.where(seen, part, -1e30) if piece == pieces - 1 else part)
        top = functools.reduce(jnp.maximum, [jnp.max(part, axis=0, keepdims=True) for part in scores])
        base = top * (scale * LOG2E)
        weights = [jnp.exp2(part * (scale * LOG2E) - base) for part in scores]
        share = 1.0 / sum(jnp.sum(part, axis=0, keepdims=True) for part in weights)
        grads = [
            lax.dot_general(
                v_in[piece * span : (piece + 1) * span, :], upstream, CONTRACT_LAST, preferred_element_type=jnp.float32
            )
            for piece in range(pieces)
        ]
        probs = [part * share for part in weights]
        delta = sum(jnp.sum(p * g, axis=0, keepdims=True) for p, g in zip(probs, grads))
        turned = None
        for piece in range(pieces):
            at_keys = slice(piece * span, (piece + 1) * span)
            dv_sum[at_keys, :] += jnp.dot(
                probs[piece].astype(jnp.bfloat16), upstream, preferred_element_type=jnp.float32
            )
            grad_scores = (probs[piece] * (grads[piece] - delta)).astype(jnp.bfloat16)
            dk_sum[at_keys, :] += jnp.dot(grad_scores, query, preferred_element_type=jnp.float32)
            part = jnp.dot(k_turned[:, at_keys], grad_scores, preferred_element_type=jnp.float32)
            turned = part if turned is None else turned + part
        dq_ref[here, :] = (turned * scale).T.astype(dq_ref.dtype)

    @pl.when(works)
    def _():
        local_wait(k_in, k_sem)
        local_wait(v_in, v_sem)
        k_turned[...] = k_in[...].T

        def take(step, carry):
            index = taken(step, s)
            local_wait(q_in.at[block(index)], q_sem.at[index])
            local_wait(g_in.at[block(index)], g_sem.at[index])
            spans = 4
            for span in range(spans):
                @pl.when(index // (parts // spans) == span)
                def _():
                    backward(index, (span + 1) * length // spans)
            return carry

        lax.fori_loop(0, parts, take, 0)

    @pl.when(no(works))
    def _():
        dq_ref[...] = jnp.zeros_like(dq_ref)

    dk_ref[...] = (dk_sum[...] * scale).astype(dk_ref.dtype)
    dv_ref[...] = dv_sum[...].astype(dv_ref.dtype)

    @pl.when(both(works, no(alone)))
    def _():
        local_wait(k_ref, k_out_sem)
        local_wait(v_ref, v_out_sem)
        local_wait(q_ref, q_out_sem)

    @pl.when(alone)
    def _():
        local_wait(q_ref.at[pl.ds(0, (parts - 1) * rows)], q_out_sem)

    @pl.when(level)
    def _():
        local_wait(q_mid, q_on_sem)

    @pl.when(gives)
    def _():
        local_wait(g_ref, g_out_sem)


def local(held_query, held_key, held_value, grad_out):
    sections, parts = lax.axis_size("section"), lax.axis_size("tp")
    _, tokens, heads, width = held_query.shape
    length = held_key.shape[1]
    group = heads // parts
    query = held_query.reshape(tokens, parts, group, width)
    query = jnp.swapaxes(query, 0, 1).reshape(parts * tokens * group, width)
    key = held_key.reshape(length, width)
    value = held_value.reshape(length, width)
    upstream = grad_out.reshape(length * group, width)
    tall, short = upstream.shape, key.shape
    grad_q, grad_k, grad_v = pl.pallas_call(
        functools.partial(kernel, sections, parts, tokens, group),
        out_shape=(
            jax.ShapeDtypeStruct(tall, jnp.bfloat16),
            jax.ShapeDtypeStruct(short, jnp.bfloat16),
            jax.ShapeDtypeStruct(short, jnp.bfloat16),
        ),
        in_specs=[pl.BlockSpec(memory_space=pl.ANY)] * 4,
        out_specs=[pl.BlockSpec(memory_space=pltpu.VMEM)] * 3,
        scratch_shapes=[
            pltpu.VMEM(tall, jnp.bfloat16),
            pltpu.VMEM(short, jnp.bfloat16),
            pltpu.VMEM(short, jnp.bfloat16),
            pltpu.VMEM(tall, jnp.bfloat16),
            pltpu.VMEM((2 * tokens * group, width), jnp.bfloat16),
            pltpu.VMEM((width, length), jnp.bfloat16),
            pltpu.VMEM(short, jnp.float32),
            pltpu.VMEM(short, jnp.float32),
            pltpu.SemaphoreType.DMA((parts,)),
            pltpu.SemaphoreType.DMA((parts,)),
        ]
        + [pltpu.SemaphoreType.DMA] * 2
        + [pltpu.SemaphoreType.DMA((2,))]
        + [pltpu.SemaphoreType.DMA] * 5
        + [pltpu.SemaphoreType.REGULAR],
        compiler_params=pltpu.CompilerParams(
            collective_id=0, has_side_effects=True, vmem_limit_bytes=48 * 1024 * 1024
        ),
    )(query, key, value, upstream)
    return (
        grad_q.reshape(grad_out.shape),
        grad_k.reshape(held_key.shape),
        grad_v.reshape(held_value.shape),
    )


def solution(mesh):
    placed = (
        P("section", "tp", None, None),
        P("section", None, "tp", None),
        P("section", None, "tp", None),
        P("section", None, "tp", None),
    )
    return jax.shard_map(
        local,
        mesh=mesh,
        in_specs=placed,
        out_specs=(
            P("section", None, "tp", None),
            P("section", None, "tp", None),
            P("section", None, "tp", None),
        ),
        check_vma=False,
    )
```

time: 106 us -> 94.2 us (0.89)
  the two profiles are of different devices: /device:TPU:38 before, /device:TPU:68 now
where the time goes in v1:
time: 94.2 us; the launch traced here: 94.1 us
  Pallas kernels  89.2 us (95%)
  local copies, waits for them, and re-layouts  4.2 us (4%)
    pallas_call x1, Pallas kernels, local(): pl.pallas_call(functools.partial(kernel, sections, parts, tokens, group),...  89.2 us
    unnamed x9, local copies, waits for them, and re-layouts  2.39 us

profile of v1, /device:TPU:68, one launch (start us, length us, event | category | flops | bytes accessed | tf_op | source)
XLA Modules:
  0.0 94.1 jit_solution(17955330536449948355)
XLA Ops:
  0.6 0.0 copy-start
  0.6 0.0 copy-start.1
  0.7 0.0 copy-start.2
  0.7 1.8 %copy.7 = bf16[64,16,4,128]{3,2,0,1:T(4,128)(2,1)S(1)} copy(bf16[64,16,4,128]{3,2,1,0:T(4,128)(2,1)} %bitcast.17) | data formatting | bytes 2097152 | tf_op jit(solution)/shard_map/reshape | solution.py:291
  2.5 0.0 copy-done
  2.5 0.0 copy-done.1
  2.5 0.0 copy-done.2
  2.5 89.2 %shard_map.67 = (bf16[4096,128]{1,0:T(8,128)(2,1)S(1)}, bf16[1024,128]{1,0:T(8,128)(2,1)S(1)}, bf16[1024,128]{1,0:T(8,128)(2,1)S(1)}) custom-call(bf16[4096,128]{1,0:T(8,128)(2,1)S(1)} %bitcast.10, bf16[1024,128]{1,0:T(8,128)(2,1)S(1)} %bitcast.13, bf16[1024,128]{1,0:T(8,128)(2,1)S(1)} %bitcast.14, bf16[4096,128]{1,0:T(8,128)(2,1)S(1)} %bitcast.11), custom_call_target="tpu_custom_call" | custom-call | tf_op jit(solution)/shard_map/pallas_call | solution.py:297
  91.7 1.0 %copy.11 = bf16[1,1024,4,128]{3,2,1,0:T(4,128)(2,1)} copy(bf16[1,1024,4,128]{3,2,1,0:T(4,128)(2,1)S(1)} %bitcast.12) | data formatting | bytes 2097152
  92.7 0.7 copy.12
  93.4 0.7 copy.13
Async XLA Ops:
  0.6 1.9 %copy-start = (bf16[1,1024,4,128]{3,2,1,0:T(4,128)(2,1)S(1)}, bf16[1,1024,4,128]{3,2,1,0:T(4,128)(2,1)}, u32[]{:S(2)}) copy-start(bf16[1,1024,4,128]{3,2,1,0:T(4,128)(2,1)} %param.7) | copy-start | bytes 3145732
  0.6 1.9 %copy-start.1 = (bf16[1,1024,1,128]{3,1,2,0:T(8,128)(2,1)S(1)}, bf16[1,1024,1,128]{3,1,2,0:T(8,128)(2,1)}, u32[]{:S(2)}) copy-start(bf16[1,1024,1,128]{3,1,2,0:T(8,128)(2,1)} %param.5) | copy-start | bytes 786436
  0.7 1.9 %copy-start.2 = (bf16[1,1024,1,128]{3,1,2,0:T(8,128)(2,1)S(1)}, bf16[1,1024,1,128]{3,1,2,0:T(8,128)(2,1)}, u32[]{:S(2)}) copy-start(bf16[1,1024,1,128]{3,1,2,0:T(8,128)(2,1)} %param.6) | copy-start | bytes 786436

commit v2 on v1

--- a/solution.py
+++ b/solution.py
@@ -12,7 +12,7 @@
 SIZE_Z = 4
 LATEST = 2
 ORDER = (0, 1, 3, 2)
-FIRST = (16, 8, 0, 4)
+FIRST = (16, 4, 0, 0)
 CONTRACT_LAST = (((1,), (1,)), ((), ()))
 
 
@@ -164,7 +164,10 @@
     def _():
         send_pair()
         lax.fori_loop(0, first, send_upstream, 0)
-        lax.fori_loop(0, size_y, send_beside, 0)
+        @pl.when(z == 0)
+        def _():
+            lax.fori_loop(0, size_y, send_beside, 0)
+
         pl.semaphore_wait(all_in, 1)
 
     lax.fori_loop(0, 2, send_round, 0)
@@ -173,6 +176,10 @@
     @pl.when(leads)
     def _():
         send_pair()
+
+    @pl.when(both(z != 0, no(leads)))
+    def _():
+        lax.fori_loop(0, size_y, send_beside, 0)
 
     lax.fori_loop(size_y, 2 * size_y, send_across, 0)
 
@@ -232,11 +239,11 @@
             dv_sum[at_keys, :] += jnp.dot(
                 probs[piece].astype(jnp.bfloat16), upstream, preferred_element_type=jnp.float32
             )
-            grad_scores = (probs[piece] * (grads[piece] - delta)).astype(jnp.bfloat16)
+            grad_scores = (probs[piece] * (grads[piece] - delta) * scale).astype(jnp.bfloat16)
             dk_sum[at_keys, :] += jnp.dot(grad_scores, query, preferred_element_type=jnp.float32)
             part = jnp.dot(k_turned[:, at_keys], grad_scores, preferred_element_type=jnp.float32)
             turned = part if turned is None else turned + part
-        dq_ref[here, :] = (turned * scale).T.astype(dq_ref.dtype)
+        dq_ref[here, :] = turned.T.astype(dq_ref.dtype)
 
     @pl.when(works)
     def _():
@@ -261,7 +268,7 @@
     def _():
         dq_ref[...] = jnp.zeros_like(dq_ref)
 
-    dk_ref[...] = (dk_sum[...] * scale).astype(dk_ref.dtype)
+    dk_ref[...] = dk_sum[...].astype(dk_ref.dtype)
     dv_ref[...] = dv_sum[...].astype(dv_ref.dtype)
 
     @pl.when(both(works, no(alone)))
@@ -281,6 +288,18 @@
     @pl.when(gives)
     def _():
         local_wait(g_ref, g_out_sem)
+
+
+def write_out(q_ref, k_ref, v_ref, dq_ref, dk_ref, dv_ref, q_sem, k_sem, v_sem):
+    copies = [
+        pltpu.make_async_copy(q_ref, dq_ref, q_sem),
+        pltpu.make_async_copy(k_ref, dk_ref, k_sem),
+        pltpu.make_async_copy(v_ref, dv_ref, v_sem),
+    ]
+    for copy in copies:
+        copy.start()
+    for copy in copies:
+        copy.wait()
 
 
 def local(held_query, held_key, held_value, grad_out):
@@ -323,6 +342,18 @@
             collective_id=0, has_side_effects=True, vmem_limit_bytes=48 * 1024 * 1024
         ),
     )(query, key, value, upstream)
+    grad_q, grad_k, grad_v = pl.pallas_call(
+        write_out,
+        out_shape=(
+            jax.ShapeDtypeStruct(tall, jnp.bfloat16),
+            jax.ShapeDtypeStruct(short, jnp.bfloat16),
+            jax.ShapeDtypeStruct(short, jnp.bfloat16),
+        ),
+        in_specs=[pl.BlockSpec(memory_space=pl.ANY)] * 3,
+        out_specs=[pl.BlockSpec(memory_space=pl.ANY)] * 3,
+        scratch_shapes=[pltpu.SemaphoreType.DMA] * 3,
+        compiler_params=pltpu.CompilerParams(vmem_limit_bytes=48 * 1024 * 1024),
+    )(grad_q, grad_k, grad_v)
     return (
         grad_q.reshape(grad_out.shape),
         grad_k.reshape(held_key.shape),

time: 94.2 us -> 91.6 us (0.972)
  the two profiles are of different devices: /device:TPU:68 before, /device:TPU:289 now
where the time goes in v2:
time: 91.6 us; the launch traced here: 91.5 us
  Pallas kernels  88.9 us (97%)
  local copies, waits for them, and re-layouts  1.83 us (2%)
    pallas_call x1, Pallas kernels, local(): pl.pallas_call(functools.partial(kernel, sections, parts, tokens, group),...  87.8 us

profile of v2, /device:TPU:289, one launch (start us, length us, event | category | flops | bytes accessed | tf_op | source)
XLA Modules:
  0.0 91.5 jit_solution(12037244531416677026)
XLA Ops:
  0.6 0.0 copy-start
  0.6 0.0 copy-start.1
  0.7 0.0 copy-start.2
  0.7 1.8 %copy.7 = bf16[64,16,4,128]{3,2,0,1:T(4,128)(2,1)S(1)} copy(bf16[64,16,4,128]{3,2,1,0:T(4,128)(2,1)} %bitcast.14) | data formatting | bytes 2097152 | tf_op jit(solution)/shard_map/reshape | solution.py:310
  2.5 0.0 copy-done
  2.5 0.0 copy-done.1
  2.5 0.0 copy-done.2
  2.5 87.8 %shard_map.67 = (bf16[4096,128]{1,0:T(8,128)(2,1)S(1)}, bf16[1024,128]{1,0:T(8,128)(2,1)S(1)}, bf16[1024,128]{1,0:T(8,128)(2,1)S(1)}) custom-call(bf16[4096,128]{1,0:T(8,128)(2,1)S(1)} %bitcast.10, bf16[1024,128]{1,0:T(8,128)(2,1)S(1)} %bitcast.12, bf16[1024,128]{1,0:T(8,128)(2,1)S(1)} %bitcast.13, bf16[4096,128]{1,0:T(8,128)(2,1)S(1)} %bitcast.11), custom_call_target="tpu_custom_call" | custom-call | tf_op jit(solution)/shard_map/pallas_call | solution.py:316
  90.3 1.2 %shard_map.68 = (bf16[4096,128]{1,0:T(8,128)(2,1)}, bf16[1024,128]{1,0:T(8,128)(2,1)}, bf16[1024,128]{1,0:T(8,128)(2,1)}) custom-call(bf16[4096,128]{1,0:T(8,128)(2,1)S(1)} %get-tuple-element.9.q_ref, bf16[1024,128]{1,0:T(8,128)(2,1)S(1)} %get-tuple-element.10.k_ref, bf16[1024,128]{1,0:T(8,128)(2,1)S(1)} %get-tuple-element.11.v_ref), custom_call_target="tpu_custom_call" | custom-call | tf_op jit(solution)/shard_map/pallas_call | solution.py:345
Async XLA Ops:
  0.6 1.9 %copy-start = (bf16[1,1024,4,128]{3,2,1,0:T(4,128)(2,1)S(1)}, bf16[1,1024,4,128]{3,2,1,0:T(4,128)(2,1)}, u32[]{:S(2)}) copy-start(bf16[1,1024,4,128]{3,2,1,0:T(4,128)(2,1)} %param.7) | copy-start | bytes 3145732
  0.6 1.9 %copy-start.1 = (bf16[1,1024,1,128]{3,1,2,0:T(8,128)(2,1)S(1)}, bf16[1,1024,1,128]{3,1,2,0:T(8,128)(2,1)}, u32[]{:S(2)}) copy-start(bf16[1,1024,1,128]{3,1,2,0:T(8,128)(2,1)} %param.5) | copy-start | bytes 786436
  0.7 1.9 %copy-start.2 = (bf16[1,1024,1,128]{3,1,2,0:T(8,128)(2,1)S(1)}, bf16[1,1024,1,128]{3,1,2,0:T(8,128)(2,1)}, u32[]{:S(2)}) copy-start(bf16[1,1024,1,128]{3,1,2,0:T(8,128)(2,1)} %param.6) | copy-start | bytes 786436

commit v3 on v2

--- a/solution.py
+++ b/solution.py
@@ -211,14 +211,17 @@
     def backward(index, keys):
         here = block(index)
         query, upstream = q_in[here, :], g_in[here, :]
-        span = length // 4
-        pieces = keys // span
-        token = index * tokens - (keys - span) + lax.broadcasted_iota(jnp.int32, (span, rows), 1) // group
-        seen = lax.broadcasted_iota(jnp.int32, (span, rows), 0) <= token
+        wide = length // 4
+        starts = list(range(0, keys, wide))
+        spans = [slice(start, min(start + wide, keys)) for start in starts]
+        pieces = len(spans)
+        edge = keys - starts[-1]
+        token = index * tokens - starts[-1] + lax.broadcasted_iota(jnp.int32, (edge, rows), 1) // group
+        seen = lax.broadcasted_iota(jnp.int32, (edge, rows), 0) <= token
         scores = []
         for piece in range(pieces):
             part = lax.dot_general(
-                k_in[piece * span : (piece + 1) * span, :], query, CONTRACT_LAST, preferred_element_type=jnp.float32
+                k_in[spans[piece], :], query, CONTRACT_LAST, preferred_element_type=jnp.float32
             )
             scores.append(jnp.where(seen, part, -1e30) if piece == pieces - 1 else part)
         top = functools.reduce(jnp.maximum, [jnp.max(part, axis=0, keepdims=True) for part in scores])
@@ -227,7 +230,7 @@
         share = 1.0 / sum(jnp.sum(part, axis=0, keepdims=True) for part in weights)
         grads = [
             lax.dot_general(
-                v_in[piece * span : (piece + 1) * span, :], upstream, CONTRACT_LAST, preferred_element_type=jnp.float32
+                v_in[spans[piece], :], upstream, CONTRACT_LAST, preferred_element_type=jnp.float32
             )
             for piece in range(pieces)
         ]
@@ -235,7 +238,7 @@
         delta = sum(jnp.sum(p * g, axis=0, keepdims=True) for p, g in zip(probs, grads))
         turned = None
         for piece in range(pieces):
-            at_keys = slice(piece * span, (piece + 1) * span)
+            at_keys = spans[piece]
             dv_sum[at_keys, :] += jnp.dot(
                 probs[piece].astype(jnp.bfloat16), upstream, preferred_element_type=jnp.float32
             )
@@ -255,7 +258,7 @@
             index = taken(step, s)
             local_wait(q_in.at[block(index)], q_sem.at[index])
             local_wait(g_in.at[block(index)], g_sem.at[index])
-            spans = 4
+            spans = 8
             for span in range(spans):
                 @pl.when(index // (parts // spans) == span)
                 def _():

time: 91.6 us -> 90.8 us (level)
  no operation moved by 1% of the time
where the time goes in v3:
time: 90.8 us; the launch traced here: 90.7 us
  Pallas kernels  88.2 us (97%)
  local copies, waits for them, and re-layouts  1.83 us (2%)
    pallas_call x1, Pallas kernels, local(): pl.pallas_call(functools.partial(kernel, sections, parts, tokens, group),...  87 us

profile of v3, /device:TPU:289, one launch (start us, length us, event | category | flops | bytes accessed | tf_op | source)
XLA Modules:
  0.0 90.7 jit_solution(440569483426205684)
XLA Ops:
  0.6 0.0 copy-start
  0.6 0.0 copy-start.1
  0.7 0.0 copy-start.2
  0.7 1.8 %copy.7 = bf16[64,16,4,128]{3,2,0,1:T(4,128)(2,1)S(1)} copy(bf16[64,16,4,128]{3,2,1,0:T(4,128)(2,1)} %bitcast.14) | data formatting | bytes 2097152 | tf_op jit(solution)/shard_map/reshape | solution.py:313
  2.5 0.0 copy-done
  2.5 0.0 copy-done.1
  2.5 0.0 copy-done.2
  2.5 87.0 %shard_map.67 = (bf16[4096,128]{1,0:T(8,128)(2,1)S(1)}, bf16[1024,128]{1,0:T(8,128)(2,1)S(1)}, bf16[1024,128]{1,0:T(8,128)(2,1)S(1)}) custom-call(bf16[4096,128]{1,0:T(8,128)(2,1)S(1)} %bitcast.10, bf16[1024,128]{1,0:T(8,128)(2,1)S(1)} %bitcast.12, bf16[1024,128]{1,0:T(8,128)(2,1)S(1)} %bitcast.13, bf16[4096,128]{1,0:T(8,128)(2,1)S(1)} %bitcast.11), custom_call_target="tpu_custom_call" | custom-call | tf_op jit(solution)/shard_map/pallas_call | solution.py:319
  89.5 1.2 %shard_map.68 = (bf16[4096,128]{1,0:T(8,128)(2,1)}, bf16[1024,128]{1,0:T(8,128)(2,1)}, bf16[1024,128]{1,0:T(8,128)(2,1)}) custom-call(bf16[4096,128]{1,0:T(8,128)(2,1)S(1)} %get-tuple-element.9.q_ref, bf16[1024,128]{1,0:T(8,128)(2,1)S(1)} %get-tuple-element.10.k_ref, bf16[1024,128]{1,0:T(8,128)(2,1)S(1)} %get-tuple-element.11.v_ref), custom_call_target="tpu_custom_call" | custom-call | tf_op jit(solution)/shard_map/pallas_call | solution.py:348
Async XLA Ops:
  0.6 1.9 %copy-start = (bf16[1,1024,4,128]{3,2,1,0:T(4,128)(2,1)S(1)}, bf16[1,1024,4,128]{3,2,1,0:T(4,128)(2,1)}, u32[]{:S(2)}) copy-start(bf16[1,1024,4,128]{3,2,1,0:T(4,128)(2,1)} %param.7) | copy-start | bytes 3145732
  0.6 1.9 %copy-start.1 = (bf16[1,1024,1,128]{3,1,2,0:T(8,128)(2,1)S(1)}, bf16[1,1024,1,128]{3,1,2,0:T(8,128)(2,1)}, u32[]{:S(2)}) copy-start(bf16[1,1024,1,128]{3,1,2,0:T(8,128)(2,1)} %param.5) | copy-start | bytes 786436
  0.7 1.9 %copy-start.2 = (bf16[1,1024,1,128]{3,1,2,0:T(8,128)(2,1)S(1)}, bf16[1,1024,1,128]{3,1,2,0:T(8,128)(2,1)}, u32[]{:S(2)}) copy-start(bf16[1,1024,1,128]{3,1,2,0:T(8,128)(2,1)} %param.6) | copy-start | bytes 786436
